TPU v7x, 32 devices: a whole 2x2x4 slice. The times are simulated.
32 devices in a mesh: dp: 8 (over z, x), band: 4 (over y, core).
Axes of the slice: x: 2, y: 2, z: 4, core: 2. Of those that a mesh axis runs over, the one named last changes fastest.
Arguments:
- tokens: bfloat16 [96, 256, 768], P('dp', 'band'), may hold values from -6 to 6
- cotangent: bfloat16 [96, 256, 768], P('dp', 'band'), may hold values from -6 to 6
- image_rows: int32 [96], P('dp'), may hold values from 10 to 16, as said below
- qkv_weight: float32 [768, 2304], P('dp', 'band'), may hold values from -0.21875 to 0.21875
- out_weight: float32 [768, 768], P('dp', 'band'), may hold values from -1.75 to 1.75
- up_weight: float32 [768, 3072], P('dp', 'band'), may hold values from -0.21875 to 0.21875
- down_weight: float32 [3072, 768], P('dp', 'band'), may hold values from -0.109375 to 0.109375
- vectors: float32 [768, 14], P('dp'), may hold values from -1.5 to 1.5, as said below
- qkv_first: float32 [768, 2304], P('dp', 'band'), may hold values from -640 to 640
- out_first: float32 [768, 768], P('dp', 'band'), may hold values from -96 to 96
- up_first: float32 [768, 3072], P('dp', 'band'), may hold values from -224 to 224
- down_first: float32 [3072, 768], P('dp', 'band'), may hold values from -448 to 448
- vector_first: float32 [768, 14], P('dp'), may hold values from -896 to 896
- qkv_second: float32 [768, 2304], P('dp', 'band'), may hold values from 4014.08 to 64225.28
- out_second: float32 [768, 768], P('dp', 'band'), may hold values from 81.92 to 1310.72
- up_second: float32 [768, 3072], P('dp', 'band'), may hold values from 512 to 8192
- down_second: float32 [3072, 768], P('dp', 'band'), may hold values from 2048 to 32768
- vector_second: float32 [768, 14], P('dp'), may hold values from 8192 to 131072
Outputs:
- layer_out: bfloat16 [96, 256, 768], P('dp', 'band')
- token_grad: float32 [96, 256, 768], P('dp', 'band')
- qkv_new: float32 [768, 2304], P('dp', 'band')
- out_new: float32 [768, 768], P('dp', 'band')
- up_new: float32 [768, 3072], P('dp', 'band')
- down_new: float32 [3072, 768], P('dp', 'band')
- vector_new: float32 [768, 14], P('dp')
- qkv_first_new: float32 [768, 2304], P('dp', 'band')
- out_first_new: float32 [768, 768], P('dp', 'band')
- up_first_new: float32 [768, 3072], P('dp', 'band')
- down_first_new: float32 [3072, 768], P('dp', 'band')
- vector_first_new: float32 [768, 14], P('dp')
- qkv_second_new: float32 [768, 2304], P('dp', 'band')
- out_second_new: float32 [768, 768], P('dp', 'band')
- up_second_new: float32 [768, 3072], P('dp', 'band')
- down_second_new: float32 [3072, 768], P('dp', 'band')
- vector_second_new: float32 [768, 14], P('dp')
- down_bias_gradient: float32 [768], P('dp')
Inputs may be any that keep to these rules, and one draw needn't show every extreme that they name: `image_rows`: each image has 10, 14 or 16 grid rows and as many grid columns; among the 12 images of each index of dp at least one has 16. `vectors`: columns 0, 5, 6 and 9 are gains and layer scales, the other columns biases.
All inputs are finite; a program needn't handle non-finite values.
Results may differ from a plain program's by a relative error of at most 0.018.
Values may be sent and summed in bfloat16 or wider, within the bound.
No kernel may reach another device: no remote copies, remote signals or barrier semaphores. Data moves between devices by JAX's collectives and lax.ppermute only.
A program may use at most 192 MiB of HBM per device.

v0:
```python
from functools import partial

import jax
import jax.numpy as jnp
from jax import lax
from jax.sharding import PartitionSpec as P

D = 768
H = 12
HD = 64
FF = 3072
GRID = 16
STEP = 7
SLOTS = 256


NORM_EPS = 1e-06
ADAM_EPS = 1e-08
BETA_ONE = 0.5
BETA_TWO = 0.6
MATRIX_DECAY = 0.05
VECTOR_RATE = 0.5
MASK_FILL = -1e30


def layer_norm(values, gain, shift):
    center = values - jnp.mean(values, axis=-1, keepdims=True)
    spread = jnp.mean(center * center, axis=-1, keepdims=True)
    return center * lax.rsqrt(spread + NORM_EPS) * gain + shift


def masked_scores(head_block, key_valid):
    scores = jnp.einsum(
        "shd,thd->hst", head_block[:, 0], head_block[:, 1], preferred_element_type=jnp.float32
    ) * HD ** (-0.5)
    return jnp.where(key_valid[None, None, :] > 0.5, scores, MASK_FILL)


def attend(packed):
    head_block, key_valid = packed
    scores = masked_scores(head_block, key_valid)
    highest = jnp.max(scores, axis=-1, keepdims=True)
    shifted = jnp.exp(scores - highest)
    totals = jnp.sum(shifted, axis=-1, keepdims=True)
    weights_low = (shifted / totals).astype(jnp.bfloat16)
    result = jnp.einsum(
        "hst,thd->shd", weights_low, head_block[:, 2], preferred_element_type=jnp.float32
    )
    return (result.astype(jnp.bfloat16), (highest + jnp.log(totals))[..., 0])


def attend_back(packed):
    head_block, log_total, grad_out, key_valid = packed
    scores = masked_scores(head_block, key_valid)
    weights_again = jnp.exp(scores - log_total[..., None])
    grad_weights = jnp.einsum(
        "shd,thd->hst", grad_out, head_block[:, 2], preferred_element_type=jnp.float32
    )
    grad_value = jnp.einsum(
        "hst,shd->thd",
        weights_again.astype(jnp.bfloat16),
        grad_out,
        preferred_element_type=jnp.float32,
    )
    center = jnp.sum(weights_again * grad_weights, axis=-1, keepdims=True)
    grad_scores = (weights_again * (grad_weights - center)).astype(jnp.bfloat16)
    grad_query = jnp.einsum(
        "hst,thd->shd", grad_scores, head_block[:, 1], preferred_element_type=jnp.float32
    ) * HD ** (-0.5)
    grad_key = jnp.einsum(
        "hst,shd->thd", grad_scores, head_block[:, 0], preferred_element_type=jnp.float32
    ) * HD ** (-0.5)
    return jnp.stack([grad_query, grad_key, grad_value], axis=1).astype(jnp.bfloat16)


def adamw_update(master, gradient, moment_one, moment_two, step_rate, weight_decay):
    first_new = BETA_ONE * moment_one + (1.0 - BETA_ONE) * gradient
    second_new = BETA_TWO * moment_two + (1.0 - BETA_TWO) * gradient * gradient
    first_hat = first_new / (1.0 - BETA_ONE**STEP)
    second_hat = second_new / (1.0 - BETA_TWO**STEP)
    master_new = master - step_rate * (
        first_hat / (jnp.sqrt(second_hat) + ADAM_EPS) + weight_decay * master
    )
    return (master_new, first_new, second_new)


def slot_valid(slot_ids, row_limit):
    inside = ((slot_ids // GRID)[None, :] < row_limit) & ((slot_ids % GRID)[None, :] < row_limit)
    return inside.astype(jnp.float32)


def on_device(
    tokens,
    cotangent,
    image_rows,
    qkv_weight,
    out_weight,
    up_weight,
    down_weight,
    vectors,
    qkv_first,
    out_first,
    up_first,
    down_first,
    vector_first,
    qkv_second,
    out_second,
    up_second,
    down_second,
    vector_second,
):
    band_count = lax.axis_size("band")
    band_index = lax.axis_index("band")
    images_here = tokens.shape[0]
    band_slots = tokens.shape[1]
    row_count = images_here * band_slots
    head_local = H // band_count
    head_span = head_local * HD
    row_limit = image_rows[:, None]
    full_valid = slot_valid(jnp.arange(SLOTS), row_limit)
    own_valid = slot_valid(band_index * band_slots + jnp.arange(band_slots), row_limit)
    row_valid = own_valid.reshape(row_count, 1)
    qkv_low = qkv_weight.astype(jnp.bfloat16)
    out_low = out_weight.astype(jnp.bfloat16)
    up_low = up_weight.astype(jnp.bfloat16)
    down_low = down_weight.astype(jnp.bfloat16)
    vector_low = vectors.astype(jnp.bfloat16)
    band_full = (
        lax.all_gather(qkv_low, "band", axis=1, tiled=True),
        lax.all_gather(out_low, "band", axis=1, tiled=True),
        lax.all_gather(up_low, "band", axis=1, tiled=True),
        lax.all_gather(down_low, "band", axis=1, tiled=True),
    )
    gathered = (
        lax.all_gather(band_full[0], "dp", axis=0, tiled=True),
        lax.all_gather(band_full[1], "dp", axis=0, tiled=True),
        lax.all_gather(band_full[2], "dp", axis=0, tiled=True),
        lax.all_gather(band_full[3], "dp", axis=0, tiled=True),
        lax.all_gather(vector_low, "dp", axis=0, tiled=True),
    )
    qkv_full, out_full, up_full, down_full, vector_full = gathered
    params = vector_full.astype(jnp.float32)
    gain_one = params[:, 0]
    shift_one = params[:, 1]
    query_bias = params[:, 2]
    value_bias = params[:, 3]
    out_bias = params[:, 4]
    scale_one = params[:, 5]
    gain_two = params[:, 6]
    shift_two = params[:, 7]
    down_bias = params[:, 8]
    scale_two = params[:, 9]
    up_bias = params[:, 10:14].T.reshape(-1)
    inputs = tokens.reshape(row_count, D).astype(jnp.float32)
    normed_one, norm_one_back = jax.vjp(layer_norm, inputs, gain_one, shift_one)
    normed_one = normed_one.astype(jnp.bfloat16)
    qkv_bias = jnp.concatenate([query_bias, jnp.zeros_like(query_bias), value_bias])
    qkv_rows = (
        jnp.dot(normed_one, qkv_full, preferred_element_type=jnp.float32) + qkv_bias
    ).astype(jnp.bfloat16)
    head_blocks = lax.all_to_all(
        qkv_rows.reshape(images_here, band_slots, 3, band_count, head_span),
        "band",
        split_axis=3,
        concat_axis=1,
        tiled=True,
    )
    head_blocks = head_blocks.reshape(images_here, SLOTS, 3, head_local, HD)
    head_out, log_totals = lax.map(attend, (head_blocks, full_valid))
    mixed_rows = lax.all_to_all(
        head_out.reshape(images_here, SLOTS, 1, head_span),
        "band",
        split_axis=1,
        concat_axis=2,
        tiled=True,
    )
    mixed_rows = mixed_rows.reshape(row_count, D)
    branch_one = jnp.dot(mixed_rows, out_full, preferred_element_type=jnp.float32) + out_bias
    middle = inputs + scale_one * branch_one
    normed_two, norm_two_back = jax.vjp(layer_norm, middle, gain_two, shift_two)
    normed_two = normed_two.astype(jnp.bfloat16)
    hidden = jnp.dot(normed_two, up_full, preferred_element_type=jnp.float32) + up_bias
    active, gelu_back = jax.vjp(partial(jax.nn.gelu, approximate=False), hidden)
    active = active.astype(jnp.bfloat16)
    branch_two = jnp.dot(active, down_full, preferred_element_type=jnp.float32) + down_bias
    layer_out = ((middle + scale_two * branch_two) * row_valid).astype(jnp.bfloat16)
    back_out = cotangent.reshape(row_count, D).astype(jnp.float32) * row_valid
    grad_branch_two = (back_out * scale_two).astype(jnp.bfloat16)
    down_grad = jnp.einsum("tf,td->fd", active, grad_branch_two, preferred_element_type=jnp.float32)
    down_bias_grad = jnp.sum(grad_branch_two.astype(jnp.float32), axis=0)
    scale_two_grad = jnp.sum(back_out * branch_two, axis=0)
    grad_active = jnp.einsum(
        "td,fd->tf", grad_branch_two, down_full, preferred_element_type=jnp.float32
    )
    grad_hidden = gelu_back(grad_active)[0].astype(jnp.bfloat16)
    up_grad = jnp.einsum("td,tf->df", normed_two, grad_hidden, preferred_element_type=jnp.float32)
    up_bias_grad = jnp.sum(grad_hidden.astype(jnp.float32), axis=0)
    grad_normed_two = jnp.einsum(
        "tf,df->td", grad_hidden, up_full, preferred_element_type=jnp.float32
    )
    grad_middle, gain_two_grad, shift_two_grad = norm_two_back(grad_normed_two)
    grad_middle = grad_middle + back_out
    grad_branch_one = (grad_middle * scale_one).astype(jnp.bfloat16)
    scale_one_grad = jnp.sum(grad_middle * branch_one, axis=0)
    out_bias_grad = jnp.sum(grad_branch_one.astype(jnp.float32), axis=0)
    out_grad = jnp.einsum(
        "td,te->de", mixed_rows, grad_branch_one, preferred_element_type=jnp.float32
    )
    grad_mixed = jnp.einsum(
        "te,de->td", grad_branch_one, out_full, preferred_element_type=jnp.float32
    ).astype(jnp.bfloat16)
    grad_heads = lax.all_to_all(
        grad_mixed.reshape(images_here, band_slots, band_count, head_span),
        "band",
        split_axis=2,
        concat_axis=1,
        tiled=True,
    )
    grad_heads = grad_heads.reshape(images_here, SLOTS, head_local, HD)
    grad_blocks = lax.map(attend_back, (head_blocks, log_totals, grad_heads, full_valid))
    grad_qkv = lax.all_to_all(
        grad_blocks.reshape(images_here, SLOTS, 3, 1, head_span),
        "band",
        split_axis=1,
        concat_axis=3,
        tiled=True,
    )
    grad_qkv = grad_qkv.reshape(row_count, 3 * D)
    qkv_grad = jnp.einsum("td,te->de", normed_one, grad_qkv, preferred_element_type=jnp.float32)
    column_sums = jnp.sum(grad_qkv.astype(jnp.float32), axis=0)
    query_bias_grad = column_sums[:D]
    value_bias_grad = column_sums[2 * D :]
    grad_normed_one = jnp.einsum(
        "te,de->td", grad_qkv, qkv_full, preferred_element_type=jnp.float32
    )
    grad_inputs, gain_one_grad, shift_one_grad = norm_one_back(grad_normed_one)
    token_grad = (grad_inputs + grad_middle).reshape(images_here, band_slots, D)
    vector_grad = jnp.concatenate(
        [
            jnp.stack(
                [
                    gain_one_grad,
                    shift_one_grad,
                    query_bias_grad,
                    value_bias_grad,
                    out_bias_grad,
                    scale_one_grad,
                    gain_two_grad,
                    shift_two_grad,
                    down_bias_grad,
                    scale_two_grad,
                ],
                axis=1,
            ),
            up_bias_grad.reshape(4, D).T,
        ],
        axis=1,
    )
    vector_total = lax.psum(vector_grad.astype(jnp.bfloat16), "band").astype(jnp.float32)
    row_part = (
        lax.psum_scatter(qkv_grad, "dp", scatter_dimension=0, tiled=True),
        lax.psum_scatter(out_grad, "dp", scatter_dimension=0, tiled=True),
        lax.psum_scatter(up_grad, "dp", scatter_dimension=0, tiled=True),
        lax.psum_scatter(down_grad, "dp", scatter_dimension=0, tiled=True),
        lax.psum_scatter(vector_total, "dp", scatter_dimension=0, tiled=True),
    )
    column_part = (
        lax.psum_scatter(
            row_part[0].astype(jnp.bfloat16), "band", scatter_dimension=1, tiled=True
        ).astype(jnp.float32),
        lax.psum_scatter(
            row_part[1].astype(jnp.bfloat16), "band", scatter_dimension=1, tiled=True
        ).astype(jnp.float32),
        lax.psum_scatter(
            row_part[2].astype(jnp.bfloat16), "band", scatter_dimension=1, tiled=True
        ).astype(jnp.float32),
        lax.psum_scatter(
            row_part[3].astype(jnp.bfloat16), "band", scatter_dimension=1, tiled=True
        ).astype(jnp.float32),
    )
    reduced = (column_part[0], column_part[1], column_part[2], column_part[3], row_part[4])
    down_bias_gradient = reduced[4][:, 8]
    qkv_new = adamw_update(qkv_weight, reduced[0], qkv_first, qkv_second, D ** (-0.5), MATRIX_DECAY)
    out_new = adamw_update(
        out_weight, reduced[1], out_first, out_second, (D // 64) ** (-0.5), MATRIX_DECAY
    )
    up_new = adamw_update(up_weight, reduced[2], up_first, up_second, D ** (-0.5), MATRIX_DECAY)
    down_new = adamw_update(
        down_weight, reduced[3], down_first, down_second, FF ** (-0.5), MATRIX_DECAY
    )
    vector_new = adamw_update(vectors, reduced[4], vector_first, vector_second, VECTOR_RATE, 0.0)
    return (
        layer_out.reshape(images_here, band_slots, D),
        token_grad,
        qkv_new[0],
        out_new[0],
        up_new[0],
        down_new[0],
        vector_new[0],
        qkv_new[1],
        out_new[1],
        up_new[1],
        down_new[1],
        vector_new[1],
        qkv_new[2],
        out_new[2],
        up_new[2],
        down_new[2],
        vector_new[2],
        down_bias_gradient,
    )


def solution(mesh):
    in_specs = (
        P("dp", "band", None),
        P("dp", "band", None),
        P("dp"),
        P("dp", "band"),
        P("dp", "band"),
        P("dp", "band"),
        P("dp", "band"),
        P("dp", None),
        P("dp", "band"),
        P("dp", "band"),
        P("dp", "band"),
        P("dp", "band"),
        P("dp", None),
        P("dp", "band"),
        P("dp", "band"),
        P("dp", "band"),
        P("dp", "band"),
        P("dp", None),
    )
    out_specs = (
        P("dp", "band", None),
        P("dp", "band", None),
        P("dp", "band"),
        P("dp", "band"),
        P("dp", "band"),
        P("dp", "band"),
        P("dp", None),
        P("dp", "band"),
        P("dp", "band"),
        P("dp", "band"),
        P("dp", "band"),
        P("dp", None),
        P("dp", "band"),
        P("dp", "band"),
        P("dp", "band"),
        P("dp", "band"),
        P("dp", None),
        P("dp"),
    )
    return jax.shard_map(
        on_device, mesh=mesh, in_specs=in_specs, out_specs=out_specs, check_vma=False
    )
```

profile of v0, /device:TPU:0, one launch (start us, length us, event | category | flops | bytes accessed | tf_op | source)
XLA Modules:
  0.0 1165.0 jit_solution(454369366186311886)
XLA Ops:
  33.1 31.2 %all-gather = bf16[8,96,14]{1,2,0:T(8,128)(2,1)S(1)} all-gather(bf16[1,96,14]{1,2,0:T(8,128)(2,1)S(1)} %convert_bitcast_fusion.1), channel_id=1, replica_groups=mesh['dp'=8,'band'=4] {'dp'}, dimensions={0}, use_global_device_ids=true | all-gather | bytes 24192 | tf_op jit(solution)/shard_map/all_gather | solution.py:139
  67.1 17.5 %all-gather.7.cloned.1.call-done = bf16[768,2304]{1,0:T(8,128)(2,1)} async-done(((bf16[96,2304]{1,0:T(8,128)(2,1)}), bf16[768,2304]{1,0:T(8,128)(2,1)}) %all-gather.7.cloned.1.call-update) | async-done | bytes 3538960 | tf_op jit(solution)/shard_map/all_gather | solution.py:135
  91.0 9.9 reshape.394
  111.5 58.1 %all_gather.34 = bf16[384,768]{0,1:T(8,128)(2,1)} all-gather(bf16[384,192]{0,1:T(8,128)(2,1)S(1)} %convert_element_type.167), channel_id=1, replica_groups=mesh['dp'=8,'band'=4] {'band'}, dimensions={1}, use_global_device_ids=true | all-gather | bytes 737280 | tf_op jit(solution)/shard_map/all_gather | solution.py:132
  169.8 10.4 copy.143
  180.2 10.9 reshape.395
  191.1 28.1 %while.22 = (s32[]{:T(128)}, bf16[12,256,3,64]{1,3,2,0:T(8,128)(2,1)S(1)}, f32[12,3,256]{2,1,0:T(4,128)}, bf16[12,256,3,3,64]{1,4,3,2,0:T(8,128)(2,1)}, f32[12,256]{1,0:T(8,128)S(1)}, /*index=5*/s32[]{:T(128)}) while((s32[]{:T(128)}, bf16[12,256,3,64]{1,3,2,0:T(8,128)(2,1)S(1)}, f32[12,3,256]{2,1,0:T(4,128)}, ...), condition=%wide.region_5.6_spmd, body=%wide.region_2.5_spmd.sunk | while | flops 51953152 | bytes 3372369 | solution.py:169
  229.5 23.6 %all-to-all-done.1 = bf16[12,256,1,192]{3,0,2,1:T(8,128)(2,1)} async-done(((bf16[12,256,1,192]{3,0,2,1:T(8,128)(2,1)}), bf16[12,256,1,192]{3,0,2,1:T(8,128)(2,1)}, u32[]{:S(2)}, u32[]{:S(2)}) %all-to-all-start.1) | async-done | bytes 1179680 | tf_op jit(solution)/shard_map/all_to_all | solution.py:170
  272.8 16.3 %all-gather.13.cloned.1.call-done = bf16[3072,768]{0,1:T(8,128)(2,1)} async-done(((bf16[384,768]{0,1:T(8,128)(2,1)}), bf16[3072,768]{0,1:T(8,128)(2,1)}) %all-gather.13.cloned.1.call-update) | async-done | bytes 4718608 | tf_op jit(solution)/shard_map/all_gather | solution.py:138
  289.1 29.6 %fusion.62 = (bf16[3072]{0:T(1024)(128)(2,1)}, bf16[768,3072]{1,0:T(8,128)(2,1)S(1)}, f32[768,3072]{1,0:T(8,128)}) fusion(f32[768,3072]{1,0:T(8,128)} %fusion.59, f32[3072]{0:T(1024)} %add.279, bf16[768,768]{1,0:T(8,128)(2,1)S(1)} %copy-done.14, bf16[3072,768]{0,1:T(8,128)(2,1)} %all-gather.13.cloned.1.call-done), kind=kOutput, calls=%fused_computation.170 | convolution fusion | flops 3798463488 | bytes 29509632 | tf_op jit(solution)/shard_map/td,fd->tf/dot_general | solution.py:192
  341.7 16.2 %all-to-all-done.2 = bf16[12,64,4,192]{3,1,0,2:T(8,128)(2,1)} async-done(((bf16[12,64,4,192]{3,1,0,2:T(8,128)(2,1)}), bf16[12,64,4,192]{3,1,0,2:T(8,128)(2,1)}, u32[]{:S(2)}, u32[]{:S(2)}) %all-to-all-start.2) | async-done | bytes 1179680 | tf_op jit(solution)/shard_map/all_to_all | solution.py:212
  365.9 56.9 %while.23 = (s32[]{:T(128)}, bf16[12,256,3,3,64]{1,4,3,2,0:T(8,128)(2,1)}, bf16[12,256,3,3,64]{1,4,3,2,0:T(8,128)(2,1)}, f32[12,256]{1,0:T(8,128)}, f32[12,3,256...) while((s32[]{:T(128)}, bf16[12,256,3,3,64]{1,4,3,2,0:T(8,128)(2,1)}, ...), condition=%wide.region_12.13_spmd, body=%wide.region_10.12_spmd.sunk | while | flops 128728576 | bytes 8079713 | solution.py:220
  439.0 68.2 %all-to-all-done.3 = bf16[12,256,3,1,192]{4,0,3,2,1:T(8,128)(2,1)} async-done(((bf16[12,256,3,1,192]{4,0,3,2,1:T(8,128)(2,1)}), bf16[12,256,3,1,192]{4,0,3,2,1:T(8,128)(2,1)}, u32[]{:S(2)}, u32[]{:S(2)}) %all-to-all-start.3) | async-done | bytes 3538976 | tf_op jit(solution)/shard_map/all_to_all | solution.py:221
  553.6 11.1 multiply_convert_fusion.1
  573.4 9.1 multiply_reduce_fusion.1
  586.3 11.1 psum.7
  609.5 53.6 %reduce-scatter.18.cloned.1.call-done = f32[96,2304]{1,0:T(8,128)} async-done(((f32[768,2304]{1,0:T(8,128)}), f32[96,2304]{1,0:T(8,128)}) %reduce-scatter.18.cloned.1.call-update) | async-done | bytes 884752 | tf_op jit(solution)/shard_map/reduce_scatter | solution.py:261
  665.4 164.0 %reduce-scatter.22.cloned.1.call-done = f32[96,3072]{1,0:T(8,128)} async-done(((f32[768,3072]{1,0:T(8,128)}), f32[96,3072]{1,0:T(8,128)}) %reduce-scatter.22.cloned.1.call-update) | async-done | bytes 1179664 | tf_op jit(solution)/shard_map/reduce_scatter | solution.py:263
  831.7 61.9 %reduce-scatter.34.cloned.1.call-done = f32[96,14]{1,0:T(8,128)} async-done(((f32[768,14]{1,0:T(8,128)}), f32[96,14]{1,0:T(8,128)}) %reduce-scatter.34.cloned.1.call-update) | async-done | bytes 5392
  894.5 165.5 %reduce-scatter.26.cloned.1.call-done = f32[384,768]{1,0:T(8,128)} async-done(((f32[3072,768]{1,0:T(8,128)}), f32[384,768]{1,0:T(8,128)}) %reduce-scatter.26.cloned.1.call-update) | async-done | bytes 1179664 | tf_op jit(solution)/shard_map/reduce_scatter | solution.py:264
  1063.6 18.2 %reduce-scatter.30.cloned.1.call-done = bf16[192,96]{1,0:T(8,128)(2,1)} async-done(((bf16[768,96]{1,0:T(8,128)(2,1)}), bf16[192,96]{1,0:T(8,128)(2,1)}) %reduce-scatter.30.cloned.1.call-update) | async-done | bytes 36880
  1083.5 23.1 %reduce-scatter.28.cloned.1.call-done = bf16[576,96]{1,0:T(8,128)(2,1)} async-done(((bf16[2304,96]{1,0:T(8,128)(2,1)}), bf16[576,96]{1,0:T(8,128)(2,1)}) %reduce-scatter.28.cloned.1.call-update) | async-done | bytes 110608
  1108.8 22.5 %reduce-scatter.24.cloned.1.call-done = bf16[96,768]{1,0:T(8,128)(2,1)} async-done(((bf16[96,3072]{1,0:T(8,128)(2,1)}), bf16[96,768]{1,0:T(8,128)(2,1)}) %reduce-scatter.24.cloned.1.call-update) | async-done | bytes 147472 | tf_op jit(solution)/shard_map/reduce_scatter | solution.py:274
  1133.3 22.7 %reduce-scatter.32.cloned.1.call-done = bf16[192,384]{1,0:T(8,128)(2,1)} async-done(((bf16[768,384]{1,0:T(8,128)(2,1)}), bf16[192,384]{1,0:T(8,128)(2,1)}) %reduce-scatter.32.cloned.1.call-update) | async-done | bytes 147472
  (473 shorter events, 294.7 us)
Async XLA Ops:
  7.2 77.4 %all-gather.7.cloned.1.call-start = ((), (), s32[]{:S(2)}) async-start(), calls=%async_computation.13 | async-start | bytes 3981312 | tf_op jit(solution)/shard_map/all_gather | solution.py:135
  18.2 240.5 %all-gather.9.cloned.1.call-start = ((), (), s32[]{:S(2)}) async-start(), calls=%async_computation.14 | async-start | bytes 1327104 | tf_op jit(solution)/shard_map/all_gather | solution.py:136
  24.8 239.0 %all-gather.11.cloned.1.call-start = ((), (), s32[]{:S(2)}) async-start(), calls=%async_computation.15 | async-start | bytes 5308416 | tf_op jit(solution)/shard_map/all_gather | solution.py:137
  106.3 63.5 %all-to-all-start = ((bf16[12,64,3,4,192]{4,1,2,0,3:T(8,128)(2,1)}), bf16[12,64,3,4,192]{4,1,2,0,3:T(8,128)(2,1)}, u32[]{:S(2)}, u32[]{:S(2)}) async-start(bf16[12,64,3,4,192]{4,1,2,0,3:T(8,128)(2,1)} %copy.142), calls=%async_computation | async-start | bytes 9437184 | tf_op jit(solution)/shard_map/all_to_all | solution.py:161
  111.4 177.6 %all-gather.13.cloned.1.call-start = ((), (), s32[]{:S(2)}) async-start(), calls=%async_computation.16 | async-start | bytes 5308416 | tf_op jit(solution)/shard_map/all_gather | solution.py:138
  222.5 30.6 %all-to-all-start.1 = ((bf16[12,256,1,192]{3,0,2,1:T(8,128)(2,1)}), bf16[12,256,1,192]{3,0,2,1:T(8,128)(2,1)}, u32[]{:S(2)}, u32[]{:S(2)}) async-start(bf16[12,256,1,192]{3,0,2,1:T(8,128)(2,1)} %copy.144), calls=%async_computation.1 | async-start | bytes 4194304 | tf_op jit(solution)/shard_map/all_to_all | solution.py:170
  333.3 24.6 %all-to-all-start.2 = ((bf16[12,64,4,192]{3,1,0,2:T(8,128)(2,1)}), bf16[12,64,4,192]{3,1,0,2:T(8,128)(2,1)}, u32[]{:S(2)}, u32[]{:S(2)}) async-start(bf16[12,64,4,192]{3,1,0,2:T(8,128)(2,1)} %copy.149), calls=%async_computation.2 | async-start | bytes 3145728 | tf_op jit(solution)/shard_map/all_to_all | solution.py:212
  337.7 269.8 %reduce-scatter.20.cloned.1.call-start = ((), (), s32[]{:S(2)}) async-start(), calls=%async_computation.18 | async-start | bytes 2654208 | tf_op jit(solution)/shard_map/reduce_scatter | solution.py:262
  431.1 76.1 %all-to-all-start.3 = ((bf16[12,256,3,1,192]{4,0,3,2,1:T(8,128)(2,1)}), bf16[12,256,3,1,192]{4,0,3,2,1:T(8,128)(2,1)}, u32[]{:S(2)}, u32[]{:S(2)}) async-start(bf16[12,256,3,1,192]{4,0,3,2,1:T(8,128)(2,1)} %copy.151), calls=%async_computation.3 | async-start | bytes 12582912 | tf_op jit(solution)/shard_map/all_to_all | solution.py:221
  436.5 226.5 %reduce-scatter.18.cloned.1.call-start = ((), (), s32[]{:S(2)}) async-start(), calls=%async_computation.17 | async-start | bytes 7962624 | tf_op jit(solution)/shard_map/reduce_scatter | solution.py:261
  536.6 292.8 %reduce-scatter.22.cloned.1.call-start = ((), (), s32[]{:S(2)}) async-start(), calls=%async_computation.19 | async-start | bytes 10616832 | tf_op jit(solution)/shard_map/reduce_scatter | solution.py:263
  546.3 347.3 %reduce-scatter.34.cloned.1.call-start = ((), (), s32[]{:S(2)}) async-start(), calls=%async_computation.25 | async-start | bytes 442368
  598.3 461.7 %reduce-scatter.26.cloned.1.call-start = ((), (), s32[]{:S(2)}) async-start(), calls=%async_computation.21 | async-start | bytes 10616832 | tf_op jit(solution)/shard_map/reduce_scatter | solution.py:264
  607.5 474.3 %reduce-scatter.30.cloned.1.call-start = ((), (), s32[]{:S(2)}) async-start(), calls=%async_computation.23 | async-start | bytes 245760
  609.4 497.2 %reduce-scatter.28.cloned.1.call-start = ((), (), s32[]{:S(2)}) async-start(), calls=%async_computation.22 | async-start | bytes 737280
  665.4 465.9 %reduce-scatter.24.cloned.1.call-start = ((), (), s32[]{:S(2)}) async-start(), calls=%async_computation.20 | async-start | bytes 737280 | tf_op jit(solution)/shard_map/reduce_scatter | solution.py:274
  831.6 231.4 %copy-start.69 = (f32[96,14]{0,1:T(8,128)S(1)}, f32[96,14]{0,1:T(8,128)}, u32[]{:S(2)}) copy-start(f32[96,14]{0,1:T(8,128)} %param.39) | copy-start | bytes 16132
  831.6 251.1 %copy-start.22 = (f32[96,192]{1,0:T(8,128)S(1)}, f32[96,192]{1,0:T(8,128)}, u32[]{:S(2)}) copy-start(f32[96,192]{1,0:T(8,128)} %param.26) | copy-start | bytes 221188
  831.6 251.1 %copy-start.32 = (f32[96,192]{1,0:T(8,128)S(1)}, f32[96,192]{1,0:T(8,128)}, u32[]{:S(2)}) copy-start(f32[96,192]{1,0:T(8,128)} %param.31) | copy-start | bytes 221188
  831.6 251.1 %copy-start.33 = (f32[96,192]{1,0:T(8,128)S(1)}, f32[96,192]{1,0:T(8,128)}, u32[]{:S(2)}) copy-start(f32[96,192]{1,0:T(8,128)} %param.36) | copy-start | bytes 221188
  831.6 276.0 %copy-start.20 = (f32[96,576]{1,0:T(8,128)S(1)}, f32[96,576]{1,0:T(8,128)}, u32[]{:S(2)}) copy-start(f32[96,576]{1,0:T(8,128)} %param.25) | copy-start | bytes 663556
  831.7 276.0 %copy-start.27 = (f32[96,576]{1,0:T(8,128)S(1)}, f32[96,576]{1,0:T(8,128)}, u32[]{:S(2)}) copy-start(f32[96,576]{1,0:T(8,128)} %param.30) | copy-start | bytes 663556
  831.7 276.0 %copy-start.28 = (f32[96,576]{1,0:T(8,128)S(1)}, f32[96,576]{1,0:T(8,128)}, u32[]{:S(2)}) copy-start(f32[96,576]{1,0:T(8,128)} %param.35) | copy-start | bytes 663556
  831.7 324.3 %reduce-scatter.32.cloned.1.call-start = ((), (), s32[]{:S(2)}) async-start(), calls=%async_computation.24 | async-start | bytes 737280
  (66 other events, 2031.4 us)
Sparse Core Ops, SparseCore 0:
  18.3 66.2 all-gather.6
  87.4 39.6 all-gather.8
  129.3 78.6 all-gather.10
  209.9 79.1 all-gather.12
  341.8 67.8 reduce-scatter.19
  536.7 126.2 reduce-scatter.17
  667.1 162.3 reduce-scatter.21
  833.0 60.5 reduce-scatter.33
  897.6 162.3 reduce-scatter.25
  1063.0 18.8 reduce-scatter.29
  1084.5 22.0 reduce-scatter.27
  1109.1 22.0 reduce-scatter.23
  1133.9 22.0 reduce-scatter.31
where the time goes:
time: 1180 us; the launch traced here: 1170 us
  waiting for transfers between devices  673 us (57%)
  local copies, waits for them, and re-layouts  140 us (12%)
  matrix products  125 us (11%)
  blocking collectives  123 us (10%)
  other arithmetic  66.9 us (6%)
  starting transfers between devices  21 us (2%)
  between operations  15.3 us (1%)
    reduce_scatter x1, waiting for transfers between devices, on_device(): lax.psum_scatter(down_grad, 'dp', scatter_dimension=0, tiled=True)  166 us
    reduce_scatter x1, waiting for transfers between devices, on_device(): lax.psum_scatter(up_grad, 'dp', scatter_dimension=0, tiled=True)  164 us
    unnamed x17, waiting for transfers between devices  126 us
    all_to_all x1, waiting for transfers between devices, on_device(): lax.all_to_all(grad_blocks.reshape(images_here, SLOTS, 3, 1, head_span),...  68.2 us
    all_gather x1, blocking collectives, on_device(): lax.all_gather(down_low, 'band', axis=1, tiled=True)  58.1 us
    reduce_scatter x1, waiting for transfers between devices, on_device(): lax.psum_scatter(qkv_grad, 'dp', scatter_dimension=0, tiled=True)  53.6 us
    all_gather x1, blocking collectives, on_device(): lax.all_gather(vector_low, 'dp', axis=0, tiled=True)  31.2 us
    dot_general x1, matrix products, on_device(): jnp.einsum('td,fd->tf', grad_branch_two, down_full, preferred_element_typ...  29.6 us
  transfers between devices with their start and end apart: 17, of which 13 were waited for; matrix products, arithmetic and copies ran while one was open for 24% of the time, Pallas kernels for 0%

commit v1 on v0

v1 whole, which is shorter than its diff:
```python
import math
from functools import partial

import jax
import jax.numpy as jnp
from jax import lax
from jax.experimental import pallas as pl
from jax.experimental.pallas import tpu as pltpu
from jax.sharding import PartitionSpec as P

D = 768
H = 12
HD = 64
FF = 3072
GRID = 16
STEP = 7
SLOTS = 256
NORM_EPS = 1e-06
ADAM_EPS = 1e-08
BETA_ONE = 0.5
BETA_TWO = 0.6
MATRIX_DECAY = 0.05
VECTOR_RATE = 0.5
MASK_FILL = -1e30
R = 768
IMGS = 3
W1 = 640
W2 = 224
F32 = jnp.float32
BF16 = jnp.bfloat16
VMEM_LIMIT = 58 * 1024 * 1024


def adamw_update(master, gradient, moment_one, moment_two, step_rate, weight_decay):
    first_new = BETA_ONE * moment_one + (1.0 - BETA_ONE) * gradient
    second_new = BETA_TWO * moment_two + (1.0 - BETA_TWO) * gradient * gradient
    first_hat = first_new / (1.0 - BETA_ONE**STEP)
    second_hat = second_new / (1.0 - BETA_TWO**STEP)
    master_new = master - step_rate * (
        first_hat / (jnp.sqrt(second_hat) + ADAM_EPS) + weight_decay * master
    )
    return (master_new, first_new, second_new)


def dot(a, b):
    return lax.dot_general(a, b, (((1,), (0,)), ((), ())), preferred_element_type=F32)


def dot_nt(a, b):
    return lax.dot_general(a, b, (((1,), (1,)), ((), ())), preferred_element_type=F32)


def dot_tn(a, b):
    return lax.dot_general(a, b, (((0,), (0,)), ((), ())), preferred_element_type=F32)


def load_all(sources, target, sems):
    span = target.shape[0] // len(sources)
    copies = [
        pltpu.make_async_copy(ref, target.at[pl.ds(k * span, span)], sems.at[k])
        for k, ref in enumerate(sources)
    ]
    for copy in copies:
        copy.start()
    return copies


def norm_parts(values):
    center = values - jnp.mean(values, axis=-1, keepdims=True)
    spread = jnp.mean(center * center, axis=-1, keepdims=True)
    inverse = lax.rsqrt(spread + NORM_EPS)
    return center * inverse, inverse


def norm_back(gy, gain, xh, inverse):
    e = gy * gain
    return inverse * (
        e - jnp.mean(e, axis=-1, keepdims=True) - xh * jnp.mean(e * xh, axis=-1, keepdims=True)
    )


def head_cut(ref, img, j):
    lane = (j % 9) * HD
    base = lane // 128 * 128
    tile = ref[j // 9, :, img, :, base : base + 128].reshape(SLOTS, 128)
    return tile[:, lane - base : lane - base + HD]


def attend_kernel(count, maps, x_ref, bias_ref, *refs):
    sources, refs = refs[:count], refs[count:]
    qkv_ref, mixed_ref, total_ref, vec_ref, weights, n1_ref, sems = refs
    copies = load_all(sources, weights, sems)
    for copy in copies:
        copy.wait()

    def block(b, i):
        return maps[b] * 8 + maps[4 + i]

    tail = jnp.concatenate([weights[block(0, i), :, 512:640] for i in range(8)], axis=0)
    table = jnp.transpose(tail.astype(F32))
    vec_ref[...] = table[64:80]
    vec = table[64:80]
    for m in range(3):
        rows = x_ref[:, m].reshape(SLOTS, D).astype(F32)
        xh, _ = norm_parts(rows)
        n1_ref[m] = (xh * vec[0:1] + vec[1:2]).astype(BF16)
    bias = jnp.concatenate([vec[2:3], jnp.zeros((1, D), F32), vec[3:4], jnp.zeros((1, 64), F32)], axis=1)
    for b in range(4):
        w = jnp.concatenate([weights[block(b, i)] for i in range(8)], axis=0)
        for m in range(3):
            part = dot(n1_ref[m], w) + bias[:, 576 * b : 576 * b + 640]
            qkv_ref[b, :, m] = part.astype(BF16).reshape(4, 64, W1)

    def image(img, carry):
        column = bias_ref[img]
        for pair in range(H // 2):
            outs = []
            for h in (2 * pair, 2 * pair + 1):
                q = head_cut(qkv_ref, img, h) * BF16(HD**-0.5)
                k = head_cut(qkv_ref, img, H + h)
                v = head_cut(qkv_ref, img, 2 * H + h)
                scores = dot_nt(k, q) + column
                highest = jnp.max(scores, axis=0, keepdims=True)
                shifted = jnp.exp(scores - highest)
                totals = jnp.sum(shifted, axis=0, keepdims=True)
                low = (shifted * (1.0 / totals)).astype(BF16)
                total_ref[img, pl.ds(h, 1), :] = highest + jnp.log(totals)
                outs.append(dot_tn(v, low))
            both = jnp.transpose(jnp.concatenate(outs, axis=0))
            mixed_ref[:, img, :, 128 * pair : 128 * pair + 128] = both.astype(BF16).reshape(4, 64, 128)
        return carry

    lax.fori_loop(0, IMGS, image, 0)


def gelu_parts(v):
    cdf = 0.5 * (1.0 + lax.erf(v * (0.5**0.5)))
    pdf = jnp.exp(v * v * -0.5) * ((2.0 * math.pi) ** -0.5)
    return v * cdf, cdf + v * pdf


def feed_kernel(count, maps, x_ref, cot_ref, mixed_ref, valid_ref, vec_ref, *refs):
    sources, refs = refs[:count], refs[count:]
    (layer_ref, middle_grad_ref, mixed_grad_ref, vec_grad_ref, keep_ref, send_ref,
     weights, grads, up, down, out, branch_ref, mid_ref, xh_ref, inv_ref, n2_ref, gb_ref, n2t_ref, gbt_ref,
     act_ref, gh_ref, br2_ref, gn2_ref, sems, out_sems) = refs
    copies = load_all(sources, weights, sems)
    for copy in copies:
        copy.wait()

    def block(b, i):
        return maps[b] * 8 + maps[4 + i]

    vec = vec_ref[...]
    for b in range(4):
        for i in range(8):
            piece = weights[block(b, i), 192:224, 0:576]
            for g in range(3):
                out[96 * i + 32 * g : 96 * i + 32 * g + 32, 192 * b : 192 * b + 192] = piece[:, 192 * g : 192 * g + 192]
    for m in range(3):
        rows = pl.ds(m * SLOTS, SLOTS)
        x = x_ref[:, m].reshape(SLOTS, D).astype(F32)
        mixed = mixed_ref[:, m].reshape(SLOTS, D)
        branch = dot(mixed, out[...]) + vec[4:5]
        branch_ref[rows] = branch
        middle = x + vec[5:6] * branch
        mid_ref[rows] = middle
        xh, inverse = norm_parts(middle)
        xh_ref[rows] = xh
        inv_ref[rows] = inverse
        n2_ref[rows] = (xh * vec[6:7] + vec[7:8]).astype(BF16)
        back = cot_ref[:, m].reshape(SLOTS, D).astype(F32) * valid_ref[m]
        gb_ref[rows] = (back * vec[9:10]).astype(BF16)
    n2t_ref[...] = jnp.transpose(n2_ref[...])
    gbt_ref[...] = jnp.transpose(gb_ref[...])
    br2_ref[...] = jnp.zeros((R, D), F32)
    gn2_ref[...] = jnp.zeros((R, D), F32)

    def tile(t, carry):
        for i in range(8):
            up[96 * i : 96 * i + 96] = weights[block(t, i), 0:96]
        for b in range(4):
            for half in range(2):
                piece = weights[block(b, 2 * t + half), 96:192]
                for e in range(2):
                    down[192 * b + 96 * e : 192 * b + 96 * e + 96, 384 * half : 384 * half + 384] = piece[
                        :, 384 * e : 384 * e + 384
                    ]
        up_bias = vec_ref[pl.ds(10 + t, 1), :]
        bias_sum = jnp.zeros((1, D), F32)
        for m in range(3):
            rows = slice(m * SLOTS, m * SLOTS + SLOTS)
            hidden = dot(n2_ref[rows], up[...]) + up_bias
            active, slope = gelu_parts(hidden)
            act_ref[rows] = active.astype(BF16)
            gh = dot(gb_ref[rows], down[...]) * slope
            low = gh.astype(BF16)
            gh_ref[rows] = low
            bias_sum += jnp.sum(low.astype(F32), axis=0, keepdims=True)
            br2_ref[rows] += dot_nt(act_ref[rows], down[...])
            gn2_ref[rows] += dot_nt(gh_ref[rows], up[...])
        vec_grad_ref[pl.ds(10 + t, 1), :] = bias_sum
        up_grad = dot(n2t_ref[...], gh_ref[...]).astype(BF16)
        for i in range(8):
            grads[block(t, i), 0:96] = up_grad[96 * i : 96 * i + 96]
        down_grad = dot(gbt_ref[...], act_ref[...]).astype(BF16)
        for b in range(4):
            for half in range(2):
                for e in range(2):
                    grads[block(b, 2 * t + half), 96:192, 384 * e : 384 * e + 384] = down_grad[
                        192 * b + 96 * e : 192 * b + 96 * e + 96, 384 * half : 384 * half + 384
                    ]
        return carry

    lax.fori_loop(0, 4, tile, 0)
    sums = [jnp.zeros((1, D), F32) for _ in range(10)]
    for m in range(3):
        rows = pl.ds(m * SLOTS, SLOTS)
        valid = valid_ref[m]
        back = cot_ref[:, m].reshape(SLOTS, D).astype(F32) * valid
        branch_two = br2_ref[rows] + vec[8:9]
        layer = (mid_ref[rows] + vec[9:10] * branch_two) * valid
        layer_ref[:, m] = layer.astype(BF16).reshape(4, 64, D)
        sums[9] += jnp.sum(back * branch_two, axis=0, keepdims=True)
        sums[8] += jnp.sum(gb_ref[rows].astype(F32), axis=0, keepdims=True)
        gy = gn2_ref[rows]
        xh = xh_ref[rows]
        sums[6] += jnp.sum(gy * xh, axis=0, keepdims=True)
        sums[7] += jnp.sum(gy, axis=0, keepdims=True)
        grad = norm_back(gy, vec[6:7], xh, inv_ref[rows]) + back
        middle_grad_ref[:, m] = grad.reshape(4, 64, D)
        sums[5] += jnp.sum(grad * branch_ref[rows], axis=0, keepdims=True)
        low = (grad * vec[5:6]).astype(BF16)
        sums[4] += jnp.sum(low.astype(F32), axis=0, keepdims=True)
        gh_ref[rows] = low
        mixed_grad_ref[:, m] = dot_nt(low, out[...]).astype(BF16).reshape(4, 64, D)
        act_ref[rows] = mixed_ref[:, m].reshape(SLOTS, D)
    vec_grad_ref[14:16] = jnp.zeros((2, D), F32)
    for k in range(10):
        vec_grad_ref[k : k + 1] = sums[k]
    out_grad = dot_tn(act_ref[...], gh_ref[...]).astype(BF16)
    for b in range(4):
        for i in range(8):
            pieces = [out_grad[96 * i + 32 * g : 96 * i + 32 * g + 32, 192 * b : 192 * b + 192] for g in range(3)]
            grads[block(b, i), 192:224] = jnp.concatenate(pieces + [jnp.zeros((32, 192), BF16)], axis=1)
    half = grads.shape[0] // 2
    puts = [
        pltpu.make_async_copy(grads.at[pl.ds(k * half, half)], ref, out_sems.at[k])
        for k, ref in enumerate((keep_ref, send_ref))
    ]
    for put in puts:
        put.start()
    for put in puts:
        put.wait()


def back_kernel(count, maps, x_ref, bias_ref, qkv_ref, total_ref, mixed_grad_ref, middle_grad_ref, vec_ref, vec_in_ref, *refs):
    sources, refs = refs[:count], refs[count:]
    token_grad_ref, keep_ref, send_ref, weights, grads, gq_ref, xh_ref, inv_ref, n1t_ref, sems, out_sems = refs
    copies = load_all(sources, weights, sems)

    def block(b, i):
        return maps[b] * 8 + maps[4 + i]

    def image(img, carry):
        column = bias_ref[img]
        parts = [None] * 36
        for h in range(H):
            q = head_cut(qkv_ref, img, h) * BF16(HD**-0.5)
            k = head_cut(qkv_ref, img, H + h)
            v = head_cut(qkv_ref, img, 2 * H + h)
            base = h // 2 * 128
            tile = mixed_grad_ref[:, img, :, base : base + 128].reshape(SLOTS, 128)
            grad_out = tile[:, h % 2 * HD : h % 2 * HD + HD]
            scores = dot_nt(k, q) + column
            again = jnp.exp(scores - total_ref[img, pl.ds(h, 1), :])
            grad_weights = dot_nt(v, grad_out)
            center = jnp.sum(again * grad_weights, axis=0, keepdims=True)
            grad_scores = (again * (grad_weights - center)).astype(BF16)
            parts[2 * H + h] = dot(again.astype(BF16), grad_out)
            parts[H + h] = dot(grad_scores, q)
            parts[h] = jnp.transpose(dot_tn(k, grad_scores)) * (HD**-0.5)
            for j in (h, H + h, 2 * H + h):
                lane = (j % 9) * HD
                gq_ref[j // 9, :, img, :, lane : lane + HD] = parts[j].astype(BF16).reshape(4, 64, HD)
        return carry

    gq_ref[:, :, :, :, 512:640] = jnp.zeros((4, 4, IMGS, 64, 128), BF16)
    lax.fori_loop(0, IMGS, image, 0)
    vec = vec_ref[...]
    for m in range(3):
        rows = pl.ds(m * SLOTS, SLOTS)
        xh, inverse = norm_parts(x_ref[:, m].reshape(SLOTS, D).astype(F32))
        xh_ref[rows] = xh
        inv_ref[rows] = inverse
        n1t_ref[:, m * SLOTS : m * SLOTS + SLOTS] = jnp.transpose((xh * vec[0:1] + vec[1:2]).astype(BF16))
    for copy in copies:
        copy.wait()
    gain_sum, shift_sum = jnp.zeros((1, D), F32), jnp.zeros((1, D), F32)
    for m in range(3):
        rows = pl.ds(m * SLOTS, SLOTS)
        gy = jnp.zeros((SLOTS, D), F32)
        for b in range(4):
            w = jnp.concatenate([weights[block(b, i)] for i in range(8)], axis=0)
            gy += dot_nt(gq_ref[b, :, m].reshape(SLOTS, W1), w)
        xh = xh_ref[rows]
        gain_sum += jnp.sum(gy * xh, axis=0, keepdims=True)
        shift_sum += jnp.sum(gy, axis=0, keepdims=True)
        grad = norm_back(gy, vec[0:1], xh, inv_ref[rows]) + middle_grad_ref[:, m].reshape(SLOTS, D)
        token_grad_ref[:, m] = grad.astype(BF16).reshape(4, 64, D)
    col = []
    for b in range(4):
        total = jnp.zeros((1, W1), F32)
        for m in range(3):
            total += jnp.sum(gq_ref[b, :, m].reshape(SLOTS, W1).astype(F32), axis=0, keepdims=True)
        col.append(total[:, :576])
    flat = jnp.concatenate(col, axis=1)
    vec_in = vec_in_ref[...]
    table = jnp.concatenate(
        [jnp.zeros((64, D), F32), gain_sum, shift_sum, flat[:, :D], flat[:, 2 * D :], vec_in[4:16], jnp.zeros((48, D), F32)], axis=0
    )
    tail = jnp.transpose(table)
    for b in range(4):
        grad_rows = jnp.concatenate([gq_ref[b, :, m].reshape(SLOTS, W1) for m in range(3)], axis=0)
        grad = dot(n1t_ref[...], grad_rows)
        last = (grad[:, 512:640] + tail).astype(BF16)
        grad = grad.astype(BF16)
        for i in range(8):
            grads[block(b, i), :, 0:512] = grad[96 * i : 96 * i + 96, 0:512]
            grads[block(b, i), :, 512:640] = last[96 * i : 96 * i + 96]
    half = grads.shape[0] // 2
    puts = [
        pltpu.make_async_copy(grads.at[pl.ds(k * half, half)], ref, out_sems.at[k])
        for k, ref in enumerate((keep_ref, send_ref))
    ]
    for put in puts:
        put.start()
    for put in puts:
        put.wait()


def swap_band(values, k):
    return lax.ppermute(values, "band", [(b, b ^ k) for b in range(lax.axis_size("band"))])


def swap_dp(values, k):
    return lax.ppermute(values, "dp", [(d, d ^ k) for d in range(lax.axis_size("dp"))])


def spread_images(values, mine):
    groups = values.reshape(4, IMGS, 64, D)
    parts = [lax.dynamic_index_in_dim(groups, mine ^ k, 0, keepdims=False) for k in range(4)]
    return jnp.stack([parts[0]] + [swap_band(parts[k], k) for k in (1, 2, 3)])


def collect_images(values, mine):
    parts = jnp.stack([values[0]] + [swap_band(values[k], k) for k in (1, 2, 3)])
    return jnp.concatenate(
        [lax.dynamic_index_in_dim(parts, mine ^ g, 0, keepdims=True) for g in range(4)]
    ).reshape(12, 64, D)


def pack_first(qkv, vectors):
    return jnp.concatenate([qkv, vectors, jnp.zeros((qkv.shape[0], W1 - 590), BF16)], axis=1)


def pack_second(up, down, out):
    turned = down.T
    lower = jnp.concatenate([turned[:96], turned[96:]], axis=1)
    spare = jnp.zeros((32, 192), BF16)
    last = jnp.concatenate([out[:32], out[32:64], out[64:96], spare], axis=1)
    return jnp.concatenate([up, lower, last], axis=0)


def unpack_second(block):
    turned = jnp.concatenate([block[96:192, :384], block[96:192, 384:]], axis=0)
    out = jnp.concatenate([block[192:, 192 * g : 192 * g + 192] for g in range(3)], axis=0)
    return block[:96], turned.T, out


def gather_blocks(shard):
    near = jnp.stack([shard] + [swap_dp(shard, 2 * k) for k in (1, 2, 3)])
    across = swap_dp(near, 1)
    beside = swap_band(near, 2)
    corner = jnp.concatenate([swap_band(across[:2], 2), swap_dp(beside[2:], 1)])
    parts = [near, across, beside, corner]
    return parts + [swap_band(part, 1) for part in parts]


def gather_blocks_full(blocks):
    parts = [blocks, swap_band(blocks, 2)]
    return parts + [swap_band(part, 1) for part in parts]


def add(*terms):
    return sum(term.astype(F32) for term in terms).astype(BF16)


def reduce_blocks(keep, send):
    shape = keep.shape[1:]
    keep = keep.reshape(2, 2, 4, *shape)
    other = swap_band(send, 1).reshape(2, 2, 4, *shape)
    from_across = swap_dp(add(keep[1, 1, :2], other[1, 1, :2]), 1)
    from_beside = swap_band(add(keep[1, 1, 2:], other[1, 1, 2:]), 2)
    beside = jnp.concatenate(
        [add(keep[1, 0, :2], other[1, 0, :2], from_across), add(keep[1, 0, 2:], other[1, 0, 2:])]
    )
    across = jnp.concatenate(
        [add(keep[0, 1, :2], other[0, 1, :2]), add(keep[0, 1, 2:], other[0, 1, 2:], from_beside)]
    )
    got_across = swap_dp(across, 1)
    got_beside = swap_band(beside, 2)
    near = [add(keep[0, 0, k], other[0, 0, k], got_across[k], got_beside[k]) for k in range(4)]
    parts = [near[0]] + [swap_dp(near[k], 2 * k) for k in (1, 2, 3)]
    return sum(part.astype(F32) for part in parts)


def reduce_blocks_full(keep, send):
    shape = keep.shape[1:]
    keep = keep.reshape(2, 8, *shape)
    other = swap_band(send, 1).reshape(2, 8, *shape)
    got = swap_band(add(keep[1], other[1]), 2)
    return add(keep[0], other[0], got)


def kernel_call(body, sources, smem, operands, out_shapes, out_spaces, scratch, flops):
    specs = [pl.BlockSpec(memory_space=pltpu.SMEM)]
    specs += [pl.BlockSpec(memory_space=pltpu.VMEM) for _ in operands]
    specs += [pl.BlockSpec(memory_space=pl.ANY) for _ in sources]
    moved = sum(v.size * v.dtype.itemsize for v in (*operands, *sources, *out_shapes))
    return pl.pallas_call(
        partial(body, len(sources)),
        out_shape=out_shapes,
        in_specs=specs,
        out_specs=tuple(pl.BlockSpec(memory_space=space) for space in out_spaces),
        scratch_shapes=scratch,
        compiler_params=pltpu.CompilerParams(vmem_limit_bytes=VMEM_LIMIT),
        cost_estimate=pl.CostEstimate(flops=flops, bytes_accessed=moved, transcendentals=0),
    )(smem, *operands, *sources)


def on_device(
    tokens, cotangent, image_rows, qkv_weight, out_weight, up_weight, down_weight, vectors,
    qkv_first, out_first, up_first, down_first, vector_first,
    qkv_second, out_second, up_second, down_second, vector_second,
):
    dp_count = lax.axis_size("dp")
    dp_mine = lax.axis_index("dp")
    mine = lax.axis_index("band")
    direct = dp_count == 8
    low = [w.astype(BF16) for w in (qkv_weight, out_weight, up_weight, down_weight, vectors)]
    if direct:
        first = gather_blocks(pack_first(low[0], low[4]))
        second = gather_blocks(pack_second(low[2], low[3], low[1]))
        flip = jnp.arange(8, dtype=jnp.int32) ^ dp_mine
        place = flip % 2 * 4 + flip // 2
    else:
        qkv_all, out_all, up_all, down_all, vec_all = [
            lax.all_gather(w, "dp", axis=0, tiled=True) for w in low
        ]
        first = jnp.stack(
            [pack_first(qkv_all[96 * i : 96 * i + 96], vec_all[96 * i : 96 * i + 96]) for i in range(8)]
        )
        second = jnp.stack(
            [
                pack_second(
                    up_all[96 * i : 96 * i + 96],
                    down_all[384 * i : 384 * i + 384],
                    out_all[96 * i : 96 * i + 96],
                )
                for i in range(8)
            ]
        )
        first = gather_blocks_full(first)
        second = gather_blocks_full(second)
        place = jnp.arange(8, dtype=jnp.int32)
    flip = jnp.arange(4, dtype=jnp.int32) ^ mine
    maps = jnp.concatenate([flip % 2 * 2 + flip // 2, place]).astype(jnp.int32)

    slots = (flip[:, None] * 64 + jnp.arange(64)[None, :]).reshape(SLOTS)
    limits = lax.dynamic_slice_in_dim(image_rows, mine * IMGS, IMGS)[:, None]
    inside = (slots // GRID < limits) & (slots % GRID < limits)
    valid = inside.astype(F32)[:, :, None]
    key_bias = jnp.where(inside, 0.0, MASK_FILL).astype(F32)[:, :, None]
    x = spread_images(tokens, mine)
    cot = spread_images(cotangent, mine)

    rows_shape = (4, IMGS, 64, D)
    sds = jax.ShapeDtypeStruct
    any_, vmem = pl.ANY, pltpu.VMEM
    qkv, mixed, totals, vec = kernel_call(
        attend_kernel, first, maps, (x, key_bias),
        (sds((4, 4, IMGS, 64, W1), BF16), sds(rows_shape, BF16), sds((IMGS, H, SLOTS), F32), sds((16, D), F32)),
        (vmem,) * 4,
        [vmem((32, 96, W1), BF16), vmem((IMGS, SLOTS, D), BF16), pltpu.SemaphoreType.DMA((8,))],
        4_000_000_000,
    )
    wide = lambda dtype: vmem((R, D), dtype)
    layer, middle_grad, mixed_grad, vec_grad, keep2, send2 = kernel_call(
        feed_kernel, second, maps, (x, cot, mixed, valid, vec),
        (sds(rows_shape, BF16), sds(rows_shape, F32), sds(rows_shape, BF16), sds((16, D), F32),
         sds((16, W2, D), BF16), sds((16, W2, D), BF16)),
        (vmem, vmem, vmem, vmem, any_, any_),
        [vmem((32, W2, D), BF16), vmem((32, W2, D), BF16), wide(BF16), wide(BF16), wide(BF16),
         wide(F32), wide(F32), wide(F32), vmem((R, 1), F32), wide(BF16), wide(BF16), wide(BF16), wide(BF16),
         wide(BF16), wide(BF16), wide(F32), wide(F32),
         pltpu.SemaphoreType.DMA((8,)), pltpu.SemaphoreType.DMA((2,))],
        24_000_000_000,
    )
    token_grad, keep1, send1 = kernel_call(
        back_kernel, first, maps, (x, key_bias, qkv, totals, mixed_grad, middle_grad, vec, vec_grad),
        (sds(rows_shape, BF16), sds((16, 96, W1), BF16), sds((16, 96, W1), BF16)),
        (vmem, any_, any_),
        [vmem((32, 96, W1), BF16), vmem((32, 96, W1), BF16), vmem((4, 4, IMGS, 64, W1), BF16),
         wide(F32), vmem((R, 1), F32), wide(BF16),
         pltpu.SemaphoreType.DMA((8,)), pltpu.SemaphoreType.DMA((2,))],
        8_000_000_000,
    )
    if direct:
        grad2 = reduce_blocks(keep2, send2)
        grad1 = reduce_blocks(keep1, send1)
        up_grad, down_grad, out_grad = unpack_second(grad2)
        qkv_grad, vector_grad = grad1[:, :576], grad1[:, 576:590]
    else:
        grad2 = reduce_blocks_full(keep2, send2)
        grad1 = reduce_blocks_full(keep1, send1)
        parts = [unpack_second(grad2[i]) for i in range(8)]
        up_grad, down_grad, out_grad = [jnp.concatenate(p) for p in zip(*parts)]
        flat = grad1.reshape(D, W1)
        up_grad, down_grad, out_grad, qkv_grad, vector_grad = [
            lax.psum_scatter(g.astype(F32), "dp", scatter_dimension=0, tiled=True)
            for g in (up_grad, down_grad, out_grad, flat[:, :576], flat[:, 576:590])
        ]
    layer_out = collect_images(layer, mine)
    token_out = collect_images(token_grad, mine).astype(F32)
    down_bias_gradient = vector_grad[:, 8]
    qkv_new = adamw_update(qkv_weight, qkv_grad, qkv_first, qkv_second, D ** (-0.5), MATRIX_DECAY)
    out_new = adamw_update(out_weight, out_grad, out_first, out_second, (D // 64) ** (-0.5), MATRIX_DECAY)
    up_new = adamw_update(up_weight, up_grad, up_first, up_second, D ** (-0.5), MATRIX_DECAY)
    down_new = adamw_update(down_weight, down_grad, down_first, down_second, FF ** (-0.5), MATRIX_DECAY)
    vector_new = adamw_update(vectors, vector_grad, vector_first, vector_second, VECTOR_RATE, 0.0)
    news = (qkv_new, out_new, up_new, down_new, vector_new)
    return (
        (layer_out, token_out)
        + tuple(n[0] for n in news)
        + tuple(n[1] for n in news)
        + tuple(n[2] for n in news)
        + (down_bias_gradient,)
    )


def solution(mesh):
    rows, matrix, table = P("dp", "band", None), P("dp", "band"), P("dp", None)
    state = (matrix, matrix, matrix, matrix, table)
    return jax.shard_map(
        on_device,
        mesh=mesh,
        in_specs=(rows, rows, P("dp")) + state + state + state,
        out_specs=(rows, rows) + state + state + state + (P("dp"),),
        check_vma=False,
    )
```

time: 1180 us -> 392 us (0.33)
  waiting for transfers between devices: 673 us -> 147 us
  matrix products: 125 us -> 0 us
  blocking collectives: 123 us -> 0 us
  Pallas kernels: 0 us -> 94 us
  local copies, waits for them, and re-layouts: 140 us -> 56.6 us
  other arithmetic: 66.9 us -> 44.4 us
  starting transfers between devices: 21 us -> 41.3 us
  between operations: 15.3 us -> 1.43 us
    reduce_scatter x5 -> x0, waiting for transfers between devices: 406 us -> none  [the longest x1 166 us: on_device(): lax.psum_scatter(down_grad, 'dp', scatter_dimension=0, tiled=True)]
    ppermute x0 -> x50, waiting for transfers between devices: none -> 147 us  [the longest x20 75.3 us: swap_dp(): lax.ppermute(values, 'dp', [(d, d ^ k) for d in range(lax.axis_size('dp'))])]
    unnamed x17 -> x0, waiting for transfers between devices: 126 us -> none
    dot_general x96 -> x0, matrix products: 125 us -> none  [the longest x1 29.6 us: on_device(): jnp.einsum('td,fd->tf', grad_branch_two, down_full, preferred_element_typ...]
    all_gather x5 -> x0, blocking collectives: 112 us -> none  [the longest x1 58.1 us: on_device(): lax.all_gather(down_low, 'band', axis=1, tiled=True)]
    all_to_all x4 -> x0, waiting for transfers between devices: 108 us -> none  [the longest x1 68.2 us: on_device(): lax.all_to_all(grad_blocks.reshape(images_here, SLOTS, 3, 1, head_span),...]
    pallas_call x0 -> x3, Pallas kernels: none -> 94 us  [kernel_call(): pl.pallas_call(partial(body, len(sources)), out_shape=out_shapes, in_spec...]
    reshape x11 -> x0, local copies, waits for them, and re-layouts: 59 us -> none  [the longest x2 15.3 us: on_device(): qkv_rows.reshape(images_here, band_slots, 3, band_count, head_span)]
  transfers between devices with their start and end apart: 17 -> 50, of which waited for: 13 -> 23; matrix products, arithmetic and copies ran while one was open for 24% -> 22% of each run, Pallas kernels for 0% -> 13%
where the time goes in v1:
time: 392 us; the launch traced here: 384 us
  waiting for transfers between devices  147 us (38%)
  Pallas kernels  94 us (24%)
  local copies, waits for them, and re-layouts  56.6 us (14%)
  other arithmetic  44.4 us (11%)
  starting transfers between devices  41.3 us (11%)
    pallas_call x3, Pallas kernels, kernel_call(): pl.pallas_call(partial(body, len(sources)), out_shape=out_shapes, in_spec...  94 us
    ppermute x20, waiting for transfers between devices, swap_dp(): lax.ppermute(values, 'dp', [(d, d ^ k) for d in range(lax.axis_size('dp'))])  75.3 us
    ppermute x30, waiting for transfers between devices, swap_band(): lax.ppermute(values, 'band', [(b, b ^ k) for b in range(lax.axis_size('ba...  71.3 us
    unnamed x114, local copies, waits for them, and re-layouts  35.4 us
    ppermute x20, starting transfers between devices, swap_dp(): lax.ppermute(values, 'dp', [(d, d ^ k) for d in range(lax.axis_size('dp'))])  25.3 us
    ppermute x30, starting transfers between devices, swap_band(): lax.ppermute(values, 'band', [(b, b ^ k) for b in range(lax.axis_size('ba...  16 us
    convert_element_type x8, other arithmetic, add(): return sum((term.astype(F32) for term in terms)).astype(BF16)  13.1 us
  transfers between devices with their start and end apart: 50, of which 23 were waited for; matrix products, arithmetic and copies ran while one was open for 22% of the time, Pallas kernels for 13%

profile of v1, /device:TPU:0, one launch (start us, length us, event | category | flops | bytes accessed | tf_op | source)
XLA Modules:
  0.0 384.3 jit_solution(1067176101343087620)
XLA Ops:
  3.7 5.1 %collective-permute-start.19 = (bf16[224,768]{1,0:T(8,128)(2,1)S(1)}, bf16[224,768]{1,0:T(8,128)(2,1)S(1)}, u32[]{:S(2)}, u32[]{:S(2)}) collective-permute-start(bf16[224,768]{1,0:T(8,128)(2,1)S(1)} %maximum_maximum_fusion), channel_id=1, source_target_pairs={{0,24},{4,28},{8,16},{12,20},{16,8},{20,12},{24,0},{28,4},{1,25},{... | collective-permute-start | bytes 1032200 | tf_op jit(solution)/shard_map/ppermute | solution.py:347
  9.5 8.3 %collective-permute-done.19 = bf16[224,768]{1,0:T(8,128)(2,1)S(1)} collective-permute-done((bf16[224,768]{1,0:T(8,128)(2,1)S(1)}, bf16[224,768]{1,0:T(8,128)(2,1)S(1)}, u32[]{:S(2)}, u32[]{:S(2)}) %collective-permute-start.19) | collective-permute-done | bytes 344096 | tf_op jit(solution)/shard_map/ppermute | solution.py:347
  17.8 20.3 %collective-permute-done.18 = bf16[224,768]{1,0:T(8,128)(2,1)S(1)} collective-permute-done((bf16[224,768]{1,0:T(8,128)(2,1)S(1)}, bf16[224,768]{1,0:T(8,128)(2,1)S(1)}, u32[]{:S(2)}, u32[]{:S(2)}) %collective-permute-start.18) | collective-permute-done | bytes 344096 | tf_op jit(solution)/shard_map/ppermute | solution.py:347
  42.4 2.5 collective-permute-start.8
  47.0 3.7 collective-permute-done.8
  50.6 3.8 collective-permute-done.7
  56.0 13.7 %collective-permute-done.20.refs_1_ = bf16[4,224,768]{2,1,0:T(8,128)(2,1)} collective-permute-done((bf16[4,224,768]{2,1,0:T(8,128)(2,1)S(1)}, bf16[4,224,768]{2,1,0:T(8,128)(2,1)}, u32[]{:S(2)}, u32[]{:S(2)}) %collective-permute-start.20) | collective-permute-done | bytes 1376288 | tf_op jit(solution)/shard_map/ppermute | solution.py:347
  70.7 2.4 collective-permute-done.21.refs_2_
  78.9 6.8 %collective-permute-done.1 = bf16[3,64,768]{2,1,0:T(8,128)(2,1)S(1)} collective-permute-done((bf16[3,64,768]{2,1,0:T(8,128)(2,1)S(1)}, bf16[3,64,768]{2,1,0:T(8,128)(2,1)S(1)}, u32[]{:S(2)}, u32[]{:S(2)}) %collective-permute-start.1) | collective-permute-done | bytes 294944 | tf_op jit(solution)/shard_map/ppermute | solution.py:343
  87.7 3.3 collective-permute-done.5
  91.9 6.5 %collective-permute-done.4 = bf16[3,64,768]{2,1,0:T(8,128)(2,1)} collective-permute-done((bf16[3,64,768]{2,1,0:T(8,128)(2,1)}, bf16[3,64,768]{2,1,0:T(8,128)(2,1)}, u32[]{:S(2)}, u32[]{:S(2)}) %collective-permute-start.4) | collective-permute-done | bytes 294944 | tf_op jit(solution)/shard_map/ppermute | solution.py:343
  98.9 22.6 %collective-permute-done.10.refs_2_ = bf16[4,96,640]{2,1,0:T(8,128)(2,1)} collective-permute-done((bf16[4,96,640]{2,1,0:T(8,128)(2,1)S(1)}, bf16[4,96,640]{2,1,0:T(8,128)(2,1)}, u32[]{:S(2)}, u32[]{:S(2)}) %collective-permute-start.10) | collective-permute-done | bytes 491552 | tf_op jit(solution)/shard_map/ppermute | solution.py:343
  143.4 21.8 %shard_map.313 = (bf16[4,4,3,64,640]{4,3,2,1,0:T(8,128)(2,1)}, bf16[4,3,64,768]{3,2,1,0:T(8,128)(2,1)}, f32[3,12,256]{2,1,0:T(8,128)}, f32[16,768]{1,0:T(8,128)}) custom-call(s32[12]{0:T(128)} %pad_add_fusion.maps, bf16[4,3,64,768]{3,2,1,0:T(8,128)(2,1)} %pad_maximum_fusion.3.x_ref, f32[3,256,1]{2,1,0:T(8,128)} %fusion.17.bias_ref, ...), custom_call_target="tpu_custom_call" | custom-call | flops 4000000000 | bytes 10312704 | tf_op jit(solution)/shard_map/pallas_call | solution.py:431
  165.2 44.3 %shard_map.314 = (bf16[4,3,64,768]{3,2,1,0:T(8,128)(2,1)}, f32[4,3,64,768]{3,2,1,0:T(8,128)}, bf16[4,3,64,768]{3,2,1,0:T(8,128)(2,1)}, f32[16,768]{1,0:T(8,128)}...) custom-call(s32[12]{0:T(128)} %pad_add_fusion.maps, bf16[4,3,64,768]{3,2,1,0:T(8,128)(2,1)} %pad_maximum_fusion.3.x_ref, ...), custom_call_target="tpu_custom_call" | custom-call | flops 24000000000 | bytes 30379008 | tf_op jit(solution)/shard_map/pallas_call | solution.py:431
  210.1 27.9 %shard_map.315 = (bf16[4,3,64,768]{3,2,1,0:T(8,128)(2,1)}, bf16[16,96,640]{2,1,0:T(8,128)(2,1)}, bf16[16,96,640]{2,1,0:T(8,128)(2,1)}) custom-call(s32[12]{0:T(128)} %pad_add_fusion.maps, bf16[4,3,64,768]{3,2,1,0:T(8,128)(2,1)} %pad_maximum_fusion.3.x_ref, f32[3,256,1]{2,1,0:T(8,128)} %fusion.17.bias_ref, ...), custom_call_target="tpu_custom_call" | custom-call | flops 8000000000 | bytes 17832960 | tf_op jit(solution)/shard_map/pallas_call | solution.py:431
  250.3 6.4 %collective-permute-done.32 = bf16[3,64,768]{2,1,0:T(8,128)(2,1)S(1)} collective-permute-done((bf16[3,64,768]{2,1,0:T(8,128)(2,1)}, bf16[3,64,768]{2,1,0:T(8,128)(2,1)S(1)}, u32[]{:S(2)}, u32[]{:S(2)}) %collective-permute-start.32) | collective-permute-done | bytes 294944 | tf_op jit(solution)/shard_map/ppermute | solution.py:343
  262.4 6.4 %collective-permute-done.29 = bf16[3,64,768]{2,1,0:T(8,128)(2,1)} collective-permute-done((bf16[3,64,768]{2,1,0:T(8,128)(2,1)}, bf16[3,64,768]{2,1,0:T(8,128)(2,1)}, u32[]{:S(2)}, u32[]{:S(2)}) %collective-permute-start.29) | collective-permute-done | bytes 294944 | tf_op jit(solution)/shard_map/ppermute | solution.py:343
  276.7 4.3 %collective-permute-done.35 = bf16[2,96,640]{2,1,0:T(8,128)(2,1)S(1)} collective-permute-done((bf16[2,96,640]{2,1,0:T(8,128)(2,1)S(1)}, bf16[2,96,640]{2,1,0:T(8,128)(2,1)S(1)}, u32[]{:S(2)}, u32[]{:S(2)}) %collective-permute-start.35) | collective-permute-done | bytes 245792 | tf_op jit(solution)/shard_map/ppermute | solution.py:343
  285.2 3.6 fusion.2
  301.9 7.7 %collective-permute-done.43 = bf16[2,224,768]{2,1,0:T(8,128)(2,1)} collective-permute-done((bf16[2,224,768]{2,1,0:T(8,128)(2,1)}, bf16[2,224,768]{2,1,0:T(8,128)(2,1)}, u32[]{:S(2)}, u32[]{:S(2)}) %collective-permute-start.43) | collective-permute-done | bytes 688160 | tf_op jit(solution)/shard_map/ppermute | solution.py:343
  310.9 2.6 fusion.1
  351.5 2.4 collective-permute-start.49
  357.1 7.3 %collective-permute-done.49 = bf16[224,768]{1,0:T(8,128)(2,1)S(1)} collective-permute-done((bf16[224,768]{1,0:T(8,128)(2,1)S(1)}, bf16[224,768]{1,0:T(8,128)(2,1)S(1)}, u32[]{:S(2)}, u32[]{:S(2)}) %collective-permute-start.49) | collective-permute-done | bytes 344096 | tf_op jit(solution)/shard_map/ppermute | solution.py:347
  364.4 15.0 %collective-permute-done.48 = bf16[224,768]{1,0:T(8,128)(2,1)S(1)} collective-permute-done((bf16[224,768]{1,0:T(8,128)(2,1)S(1)}, bf16[224,768]{1,0:T(8,128)(2,1)S(1)}, u32[]{:S(2)}, u32[]{:S(2)}) %collective-permute-start.48) | collective-permute-done | bytes 344096 | tf_op jit(solution)/shard_map/ppermute | solution.py:347
  (265 shorter events, 134.2 us)
Async XLA Ops:
  8.8 29.3 %collective-permute-start.18 = (bf16[224,768]{1,0:T(8,128)(2,1)S(1)}, bf16[224,768]{1,0:T(8,128)(2,1)S(1)}, u32[]{:S(2)}, u32[]{:S(2)}) collective-permute-start(bf16[224,768]{1,0:T(8,128)(2,1)S(1)} %maximum_maximum_fusion), channel_id=1, source_target_pairs={{0,16},{4,20},{8,24},{12,28},{16,0},{20,4},{24,8},{28,12},{1,17},{... | collective-permute-start | bytes 1032200 | tf_op jit(solution)/shard_map/ppermute | solution.py:347
  8.8 29.3 %collective-permute-start.17 = (bf16[224,768]{1,0:T(8,128)(2,1)S(1)}, bf16[224,768]{1,0:T(8,128)(2,1)S(1)}, u32[]{:S(2)}, u32[]{:S(2)}) collective-permute-start(bf16[224,768]{1,0:T(8,128)(2,1)S(1)} %maximum_maximum_fusion), channel_id=1, source_target_pairs={{0,8},{4,12},{8,0},{12,4},{16,24},{20,28},{24,16},{28,20},{1,9},{5... | collective-permute-start | bytes 1032200 | tf_op jit(solution)/shard_map/ppermute | solution.py:347
  38.3 31.4 %collective-permute-start.20 = (bf16[4,224,768]{2,1,0:T(8,128)(2,1)S(1)}, bf16[4,224,768]{2,1,0:T(8,128)(2,1)}, u32[]{:S(2)}, u32[]{:S(2)}) collective-permute-start(bf16[4,224,768]{2,1,0:T(8,128)(2,1)S(1)} %pad_maximum_fusion.refs_0_), channel_id=1, source_target_pairs={{0,4},{4,0},{8,12},{12,8},{16,20},{20,16},{24,28},{28,24},{1,5},{5... | collective-permute-start | bytes 4128776 | tf_op jit(solution)/shard_map/ppermute | solution.py:347
  39.9 33.2 %collective-permute-start.21 = (bf16[4,224,768]{2,1,0:T(8,128)(2,1)S(1)}, bf16[4,224,768]{2,1,0:T(8,128)(2,1)}, u32[]{:S(2)}, u32[]{:S(2)}) collective-permute-start(bf16[4,224,768]{2,1,0:T(8,128)(2,1)S(1)} %pad_maximum_fusion.refs_0_), channel_id=1, source_target_pairs={{0,2},{1,3},{2,0},{3,1},{4,6},{5,7},{6,4},{7,5},{8,10},{9,11},{10,... | collective-permute-start | bytes 4128776 | tf_op jit(solution)/shard_map/ppermute | solution.py:343
  50.6 27.7 %collective-permute-start.2 = (bf16[3,64,768]{2,1,0:T(8,128)(2,1)S(1)}, bf16[3,64,768]{2,1,0:T(8,128)(2,1)S(1)}, u32[]{:S(2)}, u32[]{:S(2)}) collective-permute-start(bf16[3,64,768]{2,1,0:T(8,128)(2,1)S(1)} %get-tuple-element.170), channel_id=1, source_target_pairs={{0,3},{1,2},{2,1},{3,0},{4,7},{5,6},{6,5},{7,4},{8,11},{9,10},{10,... | collective-permute-start | bytes 884744 | tf_op jit(solution)/shard_map/ppermute | solution.py:343
  54.5 31.2 %collective-permute-start.1 = (bf16[3,64,768]{2,1,0:T(8,128)(2,1)S(1)}, bf16[3,64,768]{2,1,0:T(8,128)(2,1)S(1)}, u32[]{:S(2)}, u32[]{:S(2)}) collective-permute-start(bf16[3,64,768]{2,1,0:T(8,128)(2,1)S(1)} %get-tuple-element.171), channel_id=1, source_target_pairs={{0,2},{1,3},{2,0},{3,1},{4,6},{5,7},{6,4},{7,5},{8,10},{9,11},{10,... | collective-permute-start | bytes 884744 | tf_op jit(solution)/shard_map/ppermute | solution.py:343
  55.0 32.2 %collective-permute-start = (bf16[3,64,768]{2,1,0:T(8,128)(2,1)S(1)}, bf16[3,64,768]{2,1,0:T(8,128)(2,1)S(1)}, u32[]{:S(2)}, u32[]{:S(2)}) collective-permute-start(bf16[3,64,768]{2,1,0:T(8,128)(2,1)S(1)} %get-tuple-element.172), channel_id=1, source_target_pairs={{0,1},{1,0},{2,3},{3,2},{4,5},{5,4},{6,7},{7,6},{8,9},{9,8},{10,11... | collective-permute-start | bytes 884744 | tf_op jit(solution)/shard_map/ppermute | solution.py:343
  73.1 25.3 %collective-permute-start.9 = (bf16[4,96,640]{2,1,0:T(8,128)(2,1)S(1)}, bf16[4,96,640]{2,1,0:T(8,128)(2,1)}, u32[]{:S(2)}, u32[]{:S(2)}) collective-permute-start(bf16[4,96,640]{2,1,0:T(8,128)(2,1)S(1)} %pad_maximum_fusion.9.refs_0_), channel_id=1, source_target_pairs={{0,4},{4,0},{8,12},{12,8},{16,20},{20,16},{24,28},{28,24},{1,5},{5... | collective-permute-start | bytes 1474568 | tf_op jit(solution)/shard_map/ppermute | solution.py:347
  85.6 37.8 %collective-permute-start.22 = (bf16[2,224,768]{2,1,0:T(8,128)(2,1)}, bf16[2,224,768]{2,1,0:T(8,128)(2,1)}, u32[]{:S(2)}, u32[]{:S(2)}) collective-permute-start(bf16[2,224,768]{2,1,0:T(8,128)(2,1)} %slice.336), channel_id=1, source_target_pairs={{0,2},{1,3},{2,0},{3,1},{4,6},{5,7},{6,4},{7,5},{8,10},{9,11},{10,... | collective-permute-start | bytes 2064392 | tf_op jit(solution)/shard_map/ppermute | solution.py:343
  87.2 37.9 %collective-permute-start.23 = (bf16[2,224,768]{2,1,0:T(8,128)(2,1)S(1)}, bf16[2,224,768]{2,1,0:T(8,128)(2,1)}, u32[]{:S(2)}, u32[]{:S(2)}) collective-permute-start(bf16[2,224,768]{2,1,0:T(8,128)(2,1)S(1)} %slice.337), channel_id=1, source_target_pairs={{0,4},{4,0},{8,12},{12,8},{16,20},{20,16},{24,28},{28,24},{1,5},{5... | collective-permute-start | bytes 2064392 | tf_op jit(solution)/shard_map/ppermute | solution.py:347
  91.0 30.5 %collective-permute-start.10 = (bf16[4,96,640]{2,1,0:T(8,128)(2,1)S(1)}, bf16[4,96,640]{2,1,0:T(8,128)(2,1)}, u32[]{:S(2)}, u32[]{:S(2)}) collective-permute-start(bf16[4,96,640]{2,1,0:T(8,128)(2,1)S(1)} %pad_maximum_fusion.9.refs_0_), channel_id=1, source_target_pairs={{0,2},{1,3},{2,0},{3,1},{4,6},{5,7},{6,4},{7,5},{8,10},{9,11},{10,... | collective-permute-start | bytes 1474568 | tf_op jit(solution)/shard_map/ppermute | solution.py:343
  98.4 31.4 %collective-permute-start.13 = (bf16[4,96,640]{2,1,0:T(8,128)(2,1)S(1)}, bf16[4,96,640]{2,1,0:T(8,128)(2,1)}, u32[]{:S(2)}, u32[]{:S(2)}) collective-permute-start(bf16[4,96,640]{2,1,0:T(8,128)(2,1)S(1)} %pad_maximum_fusion.9.refs_0_), channel_id=1, source_target_pairs={{0,1},{1,0},{2,3},{3,2},{4,5},{5,4},{6,7},{7,6},{8,9},{9,8},{10,11... | collective-permute-start | bytes 1474568 | tf_op jit(solution)/shard_map/ppermute | solution.py:343
  98.4 34.9 %collective-permute-start.14 = (bf16[4,96,640]{2,1,0:T(8,128)(2,1)}, bf16[4,96,640]{2,1,0:T(8,128)(2,1)}, u32[]{:S(2)}, u32[]{:S(2)}) collective-permute-start(bf16[4,96,640]{2,1,0:T(8,128)(2,1)} %collective-permute-done.9.refs_1_), channel_id=1, source_target_pairs={{0,1},{1,0},{2,3},{3,2},{4,5},{5,4},{6,7},{7,6},{8,9},{9,8},{10,11... | collective-permute-start | bytes 1474568 | tf_op jit(solution)/shard_map/ppermute | solution.py:343
  129.7 35.5 %collective-permute-start.24 = (bf16[4,224,768]{2,1,0:T(8,128)(2,1)S(1)}, bf16[4,224,768]{2,1,0:T(8,128)(2,1)}, u32[]{:S(2)}, u32[]{:S(2)}) collective-permute-start(bf16[4,224,768]{2,1,0:T(8,128)(2,1)S(1)} %pad_maximum_fusion.refs_0_), channel_id=1, source_target_pairs={{0,1},{1,0},{2,3},{3,2},{4,5},{5,4},{6,7},{7,6},{8,9},{9,8},{10,11... | collective-permute-start | bytes 4128776 | tf_op jit(solution)/shard_map/ppermute | solution.py:343
  132.0 33.2 %collective-permute-start.25 = (bf16[4,224,768]{2,1,0:T(8,128)(2,1)}, bf16[4,224,768]{2,1,0:T(8,128)(2,1)}, u32[]{:S(2)}, u32[]{:S(2)}) collective-permute-start(bf16[4,224,768]{2,1,0:T(8,128)(2,1)} %collective-permute-done.20.refs_1_), channel_id=1, source_target_pairs={{0,1},{1,0},{2,3},{3,2},{4,5},{5,4},{6,7},{7,6},{8,9},{9,8},{10,11... | collective-permute-start | bytes 4128776 | tf_op jit(solution)/shard_map/ppermute | solution.py:343
  133.3 32.0 %collective-permute-start.26 = (bf16[4,224,768]{2,1,0:T(8,128)(2,1)}, bf16[4,224,768]{2,1,0:T(8,128)(2,1)}, u32[]{:S(2)}, u32[]{:S(2)}) collective-permute-start(bf16[4,224,768]{2,1,0:T(8,128)(2,1)} %collective-permute-done.21.refs_2_), channel_id=1, source_target_pairs={{0,1},{1,0},{2,3},{3,2},{4,5},{5,4},{6,7},{7,6},{8,9},{9,8},{10,11... | collective-permute-start | bytes 4128776 | tf_op jit(solution)/shard_map/ppermute | solution.py:343
  133.3 32.0 %collective-permute-start.27 = (bf16[4,224,768]{2,1,0:T(8,128)(2,1)}, bf16[4,224,768]{2,1,0:T(8,128)(2,1)}, u32[]{:S(2)}, u32[]{:S(2)}) collective-permute-start(bf16[4,224,768]{2,1,0:T(8,128)(2,1)} %constant_dynamic-update-slice_fusion.2.refs_3_), channel_id=1, source_target_pairs={{0,1},{1,0},{2,3},{3,2},{4,5},{5,4},{6,7},{7,6},{8,9},{9,8},{10,11... | collective-permute-start | bytes 4128776 | tf_op jit(solution)/shard_map/ppermute | solution.py:343
  209.6 75.7 %collective-permute-start.42 = (bf16[16,224,768]{2,1,0:T(8,128)(2,1)}, bf16[16,224,768]{2,1,0:T(8,128)(2,1)}, u32[]{:S(2)}, u32[]{:S(2)}) collective-permute-start(bf16[16,224,768]{2,1,0:T(8,128)(2,1)} %get-tuple-element.43), channel_id=1, source_target_pairs={{0,1},{1,0},{2,3},{3,2},{4,5},{5,4},{6,7},{7,6},{8,9},{9,8},{10,11... | collective-permute-start | bytes 16515080 | tf_op jit(solution)/shard_map/ppermute | solution.py:343
  238.0 33.4 %collective-permute-start.34 = (bf16[16,96,640]{2,1,0:T(8,128)(2,1)}, bf16[16,96,640]{2,1,0:T(8,128)(2,1)S(1)}, u32[]{:S(2)}, u32[]{:S(2)}) collective-permute-start(bf16[16,96,640]{2,1,0:T(8,128)(2,1)} %get-tuple-element.41), channel_id=1, source_target_pairs={{0,1},{1,0},{2,3},{3,2},{4,5},{5,4},{6,7},{7,6},{8,9},{9,8},{10,11... | collective-permute-start | bytes 5898248 | tf_op jit(solution)/shard_map/ppermute | solution.py:343
  314.7 34.7 %collective-permute-start.46 = (bf16[4,224,768]{2,1,0:T(8,128)(2,1)}, bf16[4,224,768]{2,1,0:T(8,128)(2,1)S(1)}, u32[]{:S(2)}, u32[]{:S(2)}) collective-permute-start(bf16[4,224,768]{2,1,0:T(8,128)(2,1)} %pad_maximum_fusion.2), channel_id=1, source_target_pairs={{0,2},{1,3},{2,0},{3,1},{4,6},{5,7},{6,4},{7,5},{8,10},{9,11},{10,... | collective-permute-start | bytes 4128776 | tf_op jit(solution)/shard_map/ppermute | solution.py:343
  317.3 32.2 %collective-permute-start.44 = (bf16[4,224,768]{2,1,0:T(8,128)(2,1)}, bf16[4,224,768]{2,1,0:T(8,128)(2,1)S(1)}, u32[]{:S(2)}, u32[]{:S(2)}) collective-permute-start(bf16[4,224,768]{2,1,0:T(8,128)(2,1)} %pad_maximum_fusion.1), channel_id=1, source_target_pairs={{0,4},{4,0},{8,12},{12,8},{16,20},{20,16},{24,28},{28,24},{1,5},{5... | collective-permute-start | bytes 4128776 | tf_op jit(solution)/shard_map/ppermute | solution.py:347
  318.6 21.7 %collective-permute-start.41 = (bf16[96,640]{0,1:T(8,128)(2,1)}, bf16[96,640]{0,1:T(8,128)(2,1)}, u32[]{:S(2)}, u32[]{:S(2)}) collective-permute-start(bf16[96,640]{0,1:T(8,128)(2,1)} %fusion.12), channel_id=1, source_target_pairs={{0,24},{4,28},{8,16},{12,20},{16,8},{20,12},{24,0},{28,4},{1,25},{... | collective-permute-start | bytes 368648 | tf_op jit(solution)/shard_map/ppermute | solution.py:347
  353.9 25.4 %collective-permute-start.48 = (bf16[224,768]{1,0:T(8,128)(2,1)S(1)}, bf16[224,768]{1,0:T(8,128)(2,1)S(1)}, u32[]{:S(2)}, u32[]{:S(2)}) collective-permute-start(bf16[224,768]{1,0:T(8,128)(2,1)S(1)} %get-tuple-element.128), channel_id=1, source_target_pairs={{0,16},{4,20},{8,24},{12,28},{16,0},{20,4},{24,8},{28,12},{1,17},{... | collective-permute-start | bytes 1032200 | tf_op jit(solution)/shard_map/ppermute | solution.py:347
  353.9 25.4 %collective-permute-start.47 = (bf16[224,768]{1,0:T(8,128)(2,1)S(1)}, bf16[224,768]{1,0:T(8,128)(2,1)S(1)}, u32[]{:S(2)}, u32[]{:S(2)}) collective-permute-start(bf16[224,768]{1,0:T(8,128)(2,1)S(1)} %get-tuple-element.126), channel_id=1, source_target_pairs={{0,8},{4,12},{8,0},{12,4},{16,24},{20,28},{24,16},{28,20},{1,9},{5... | collective-permute-start | bytes 1032200 | tf_op jit(solution)/shard_map/ppermute | solution.py:347
  (71 other events, 733.3 us)
